TPU v7x, 32 devices: a whole 2x2x4 slice. The times are simulated.
32 devices in a mesh: parts: 2 (over x), dp: 16 (over z, y, core).
Axes of the slice: x: 2, y: 2, z: 4, core: 2. Of those that a mesh axis runs over, the one named last changes fastest.
Arguments:
- train_grads: bfloat16 [16384, 4096], P(('parts', 'dp')), parts along dimension 0, may hold values from -160 to 160
- query_grads: bfloat16 [768, 4096], P(('parts', 'dp')), parts along dimension 0, may hold values from -0.29882812 to 0.29882812
- in_basis: bfloat16 [4, 32, 32], replicated, may hold values from -1 to 1
- out_basis: bfloat16 [4, 32, 32], replicated, may hold values from -1 to 1
- damping: float32 [2], replicated, may hold values from 0.05 to 1
- layer_group: int32 [4], replicated, may hold values from 0 to 1, as said below
Outputs:
- scores: float32 [16384, 384], P(('parts', 'dp')), parts along dimension 0
There are 2 independent parts, one for each index of `parts`. A program takes and returns all parts, laid end to end along the dimension named above; an argument that names none is the same for every part. Nothing has to cross between parts.
Inputs may be any that keep to these rules, and one draw needn't show every extreme that they name: `layer_group`: every group holds at least one layer.
All inputs are finite; a program needn't handle non-finite values.
Results may differ from a plain program's by a relative error of at most 0.0065.
Values may be sent and summed in bfloat16 or wider, within the bound.
A program may use at most 128 MiB of HBM per device.

v0:
```python
import functools

import jax
import jax.numpy as jnp
from jax import lax
from jax.experimental import pallas as pl
from jax.experimental.pallas import tpu as pltpu
from jax.sharding import PartitionSpec as P

F32 = jnp.float32
BF16 = jnp.bfloat16
CORES = 2
LINES = 2
TRANS = (((1,), (1,)), ((), ()))


def kernel(
    dp, count, train, query, in_basis, out_basis, damping, layer_group, out,
    rows_in, gathered, basis, rotated, scaled, near, far,
    train_sem, own_sem, u_send, u_recv, d_send, d_recv, y_send, y_recv, c_send, c_recv,
    near_send, near_recv, far_send, far_recv,
):
    layers, rows, size = rows_in.shape
    width = in_basis.shape[1]
    depth = dp // (CORES * LINES)
    queries = gathered.shape[1] * gathered.shape[2]
    tile = 256
    me = lax.axis_index("dp")
    c = lax.rem(me, CORES)
    y = lax.rem(me // CORES, LINES)
    z = me // (CORES * LINES)

    def device(z_, y_, c_):
        return (z_ * LINES + y_) * CORES + c_

    def behind(k):
        return lax.rem(z + depth - k, depth)

    def ahead(k):
        return lax.rem(z + k, depth)

    other_y = 1 - y
    other_c = 1 - c

    def columns(ch):
        return pl.ds(pl.multiple_of(ch * size, size), size)

    def mate(j):
        return device(z, lax.rem(y + j // CORES, LINES), lax.rem(c + j % CORES, CORES))

    def remote(src, dst, send, recv, to):
        return pltpu.make_async_remote_copy(
            src_ref=src, dst_ref=dst, send_sem=send, recv_sem=recv,
            device_id={"dp": to}, device_id_type=pl.DeviceIdType.MESH,
        )

    def load(l):
        return pltpu.make_async_copy(train.at[:, columns(l)], rows_in.at[l], train_sem.at[l])

    def own(ch):
        return pltpu.make_async_copy(query.at[:, columns(ch)], gathered.at[ch, me], own_sem.at[ch])

    def up_copy(ch, m, slot):
        return remote(gathered.at[ch, slot], gathered.at[ch, slot], u_send.at[ch, m], u_recv.at[ch, m],
                      device(z + 1, y, c))

    def down_copy(ch, m, slot):
        return remote(gathered.at[ch, slot], gathered.at[ch, slot], d_send.at[ch, m], d_recv.at[ch, m],
                      device(z - 1, y, c))

    def y_copy(ch, k, slot):
        return remote(gathered.at[ch, slot], gathered.at[ch, slot], y_send.at[ch, k], y_recv.at[ch, k],
                      device(z, other_y, c))

    def c_copy(ch, line, k, slot):
        return remote(gathered.at[ch, slot], gathered.at[ch, slot], c_send.at[ch, line, k],
                      c_recv.at[ch, line, k], device(z, y, other_c))

    for l in range(layers):
        load(l).start()
    for ch in range(layers):
        own(ch).start()

    barrier = pltpu.get_barrier_semaphore()

    def greet(k, carry):
        pl.semaphore_signal(barrier, inc=1, device_id={"dp": device(ahead(k), y, c)},
                            device_id_type=pl.DeviceIdType.MESH)
        return carry

    lax.fori_loop(1, depth, greet, 0)
    for j in range(1, CORES * LINES):
        pl.semaphore_signal(barrier, inc=1, device_id={"dp": mate(j)}, device_id_type=pl.DeviceIdType.MESH)
    pl.semaphore_wait(barrier, depth - 1 + CORES * LINES - 1)

    below = z > 0
    above = z < depth - 1

    def begin(ch, carry):
        own(ch).wait()

        @pl.when(above)
        def _():
            up_copy(ch, 1, me).start()

        @pl.when(below)
        def _():
            down_copy(ch, 1, me).start()

        y_copy(ch, 0, me).start()
        c_copy(ch, 0, 0, me).start()
        return carry

    lax.fori_loop(0, layers, begin, 0)

    def hop(step):
        m, ch = step // layers + 1, lax.rem(step, layers)

        @pl.when(z >= m)
        def _():
            slot = device(z - m, y, c)
            up_copy(ch, m, slot).wait_recv()

            @pl.when(above)
            def _():
                up_copy(ch, m + 1, slot).start()

            y_copy(ch, m, slot).start()
            c_copy(ch, 0, m, slot).start()

        @pl.when(z + m < depth)
        def _():
            slot = device(z + m, y, c)
            down_copy(ch, m, slot).wait_recv()

            @pl.when(below)
            def _():
                down_copy(ch, m + 1, slot).start()

            y_copy(ch, depth - m, slot).start()
            c_copy(ch, 0, depth - m, slot).start()

    def cross(step):
        m, ch = step // layers, lax.rem(step, layers)

        @pl.when(z >= m)
        def _():
            slot = device(z - m, other_y, c)
            y_copy(ch, m, slot).wait_recv()
            c_copy(ch, 1, m, slot).start()

        @pl.when(jnp.logical_and(m > 0, z + m < depth))
        def _():
            slot = device(z + m, other_y, c)
            y_copy(ch, depth - m, slot).wait_recv()
            c_copy(ch, 1, depth - m, slot).start()

    def run(move, start, count_):
        def step(i, carry):
            move(start + i)
            return carry

        lax.fori_loop(0, count_, step, 0)

    def arrive(ch):
        def step(k, carry):
            c_copy(ch, 0, k, device(behind(k), y, other_c)).wait_recv()
            c_copy(ch, 1, k, device(behind(k), other_y, other_c)).wait_recv()
            return carry

        lax.fori_loop(0, depth, step, 0)

    lane = lax.broadcasted_iota(jnp.int32, (width, size), 1)
    line = lax.broadcasted_iota(jnp.int32, (width, size), 0)
    spread_out = jnp.where(lane // width == line, 1.0, 0.0).astype(BF16)
    spread_in = jnp.where(lane % width == line, 1.0, 0.0).astype(BF16)

    def near_copy(j, l):
        return remote(near.at[0, l], near.at[j, l], near_send.at[j, l], near_recv.at[j, l], mate(j))

    def far_copy(k, l):
        return remote(far.at[0, l], far.at[k, l], far_send.at[k, l], far_recv.at[k, l], device(ahead(k), y, c))

    def send_far(l):
        total = near[0, l]
        for j in range(1, CORES * LINES):
            near_copy(j, l).wait_recv()
            total = total + near[j, l]
        far[0, l] = total

        def step(k, carry):
            far_copy(k, l).start()
            return carry

        lax.fori_loop(1, depth, step, 0)

    def take_far(l):
        def step(k, total):
            far_copy(k, l).wait_recv()
            return total + far[k, l]

        row = lax.fori_loop(1, depth, step, far[0, l]) * (1.0 / count)
        damp = 0.0
        for g in range(damping.shape[0]):
            damp = damp + jnp.where(layer_group[l] == g, damping[g], 0.0)
        return 1.0 / (row + damp * jnp.mean(row, axis=1, keepdims=True))

    hops = (depth - 1) * 2 // 3
    late_hops = depth - 1 - hops
    crosses = depth // 4
    late_crosses = depth - crosses

    def rotate(l, carry):
        outer = jnp.dot(out_basis[l], spread_out, preferred_element_type=F32)
        inner = jnp.dot(in_basis[l], spread_in, preferred_element_type=F32)
        for i in range(width):
            basis[l, i * width:(i + 1) * width, :] = (outer[i:i + 1, :] * inner).astype(BF16)
        load(l).wait()
        for n in range(size // tile):
            cols = slice(n * tile, (n + 1) * tile)
            part = jnp.dot(rows_in[l], basis[l, :, cols], preferred_element_type=F32)
            rotated[l, :, cols] = part
            near[0, l, :, cols] = jnp.sum(part * part, axis=0, keepdims=True)
        for j in range(1, CORES * LINES):
            near_copy(j, l).start()
        run(hop, l * hops, hops)

        @pl.when(l > 0)
        def _():
            send_far(l - 1)

        run(cross, l * crosses, crosses)
        return carry

    lax.fori_loop(0, layers, rotate, 0)
    send_far(layers - 1)

    def back(l, carry):
        scaled[...] = (rotated[l] * take_far(l)).astype(BF16)
        for n in range(size // tile):
            cols = slice(n * tile, (n + 1) * tile)
            part = lax.dot_general(scaled[...], basis[l, cols, :], TRANS, preferred_element_type=F32)
            rows_in[l, :, cols] = part.astype(BF16)
        run(hop, layers * hops + l * late_hops, late_hops)
        run(cross, layers * crosses + l * late_crosses, late_crosses)
        return carry

    lax.fori_loop(0, layers, back, 0)

    for ch in range(layers):
        arrive(ch)
        block = gathered[ch].astype(F32).reshape(queries, size).astype(BF16)
        term = lax.dot_general(rows_in[ch], block, TRANS, preferred_element_type=F32)
        if ch == 0:
            out[...] = term
        else:
            out[...] += term

    def finish(ch, carry):
        def step(k, inner):
            y_copy(ch, k, me).wait_send()
            c_copy(ch, 0, k, me).wait_send()
            c_copy(ch, 1, k, me).wait_send()
            return inner

        def step_z(m, inner):
            @pl.when(jnp.logical_and(above, z + 1 >= m))
            def _():
                up_copy(ch, m, me).wait_send()

            @pl.when(jnp.logical_and(below, z - 1 + m < depth))
            def _():
                down_copy(ch, m, me).wait_send()

            far_copy(m, ch).wait_send()
            return inner

        lax.fori_loop(0, depth, step, 0)
        lax.fori_loop(1, depth, step_z, 0)
        for j in range(1, CORES * LINES):
            near_copy(j, ch).wait_send()
        return carry

    lax.fori_loop(0, layers, finish, 0)


def per_device(dp, train_grads, query_grads, in_basis, out_basis, damping, layer_group):
    layers, width, _ = in_basis.shape
    rows = train_grads.shape[0]
    each = query_grads.shape[0]
    size = width * width
    depth = dp // (CORES * LINES)
    dma = pltpu.SemaphoreType.DMA
    vmem = pl.BlockSpec(memory_space=pltpu.VMEM)
    smem = pl.BlockSpec(memory_space=pltpu.SMEM)
    anywhere = pl.BlockSpec(memory_space=pl.ANY)
    return pl.pallas_call(
        functools.partial(kernel, dp, float(rows * dp)),
        out_shape=jax.ShapeDtypeStruct((rows, each * dp), F32),
        in_specs=[anywhere, anywhere, vmem, vmem, smem, smem],
        out_specs=vmem,
        scratch_shapes=[
            pltpu.VMEM((layers, rows, size), BF16),
            pltpu.VMEM((layers, dp, each, size), BF16),
            pltpu.VMEM((layers, size, size), BF16),
            pltpu.VMEM((layers, rows, size), F32),
            pltpu.VMEM((rows, size), BF16),
            pltpu.VMEM((CORES * LINES, layers, 1, size), F32),
            pltpu.VMEM((depth, layers, 1, size), F32),
            dma((layers,)), dma((layers,)),
            dma((layers, depth)), dma((layers, depth)),
            dma((layers, depth)), dma((layers, depth)),
            dma((layers, depth)), dma((layers, depth)),
            dma((layers, LINES, depth)), dma((layers, LINES, depth)),
            dma((CORES * LINES, layers)), dma((CORES * LINES, layers)),
            dma((depth, layers)), dma((depth, layers)),
        ],
        compiler_params=pltpu.CompilerParams(
            collective_id=0, has_side_effects=True, vmem_limit_bytes=56 * 1024 * 1024
        ),
        name="scores",
    )(train_grads, query_grads, in_basis, out_basis, damping, layer_group)


def solution(mesh):
    placed = (P(("parts", "dp"), None), P(("parts", "dp"), None), P(), P(), P(), P())
    return jax.shard_map(
        functools.partial(per_device, mesh.shape["dp"]),
        mesh=mesh, in_specs=placed, out_specs=P(("parts", "dp"), None), check_vma=False,
    )
```

profile of v0, /device:TPU:0, one launch (start us, length us, event | category | flops | bytes accessed | tf_op | source)
XLA Modules:
  0.0 38.8 jit_solution(13651671549532920296)
XLA Ops:
  0.0 36.7 %scores.1 = f32[512,384]{1,0:T(8,128)} custom-call(bf16[512,4096]{1,0:T(8,128)(2,1)} %train.1, bf16[24,4096]{1,0:T(8,128)(2,1)} %query.1, bf16[4,32,32]{2,1,0:T(8,128)(2,1)} %in_basis.1, bf16[4,32,32]{2,1,0:T(8,128)(2,1)} %out_basis.1, f32[2]{0:T(128)} %damping.1, s32[4]{0:T(128)} %layer_group.1), custom_call_target="tpu_custom_call" | custom-call | tf_op jit(solution)/shard_map/scores/pallas_call | solution.py:297
  36.7 2.1 %copy.8 = f32[512,384]{1,0:T(8,128)} copy(f32[512,384]{1,0:T(8,128)} %scores.1) | data formatting | bytes 1572864
where the time goes:
time: 39 us; the launch traced here: 38.8 us
  Pallas kernels  36.7 us (94%)
  local copies, waits for them, and re-layouts  2.06 us (5%)
    pallas_call x1, Pallas kernels, per_device(): pl.pallas_call(functools.partial(kernel, dp, float(rows * dp)), out_shape...  36.7 us
    unnamed x1, local copies, waits for them, and re-layouts  2.06 us

commit v1 on v0

--- a/solution.py
+++ b/solution.py
@@ -205,9 +205,9 @@
             damp = damp + jnp.where(layer_group[l] == g, damping[g], 0.0)
         return 1.0 / (row + damp * jnp.mean(row, axis=1, keepdims=True))
 
-    hops = (depth - 1) * 2 // 3
+    hops = depth - 1
     late_hops = depth - 1 - hops
-    crosses = depth // 4
+    crosses = depth // 2
     late_crosses = depth - crosses
 
     def rotate(l, carry):

time: 39 us -> 37.9 us (0.972)
  Pallas kernels: 36.7 us -> 35.6 us
    pallas_call x1, Pallas kernels: 36.7 us -> 35.6 us  [per_device(): pl.pallas_call(functools.partial(kernel, dp, float(rows * dp)), out_shape...]
where the time goes in v1:
time: 37.9 us; the launch traced here: 37.6 us
  Pallas kernels  35.6 us (94%)
  local copies, waits for them, and re-layouts  2.06 us (5%)
    pallas_call x1, Pallas kernels, per_device(): pl.pallas_call(functools.partial(kernel, dp, float(rows * dp)), out_shape...  35.6 us
    unnamed x1, local copies, waits for them, and re-layouts  2.06 us

profile of v1, /device:TPU:0, one launch (start us, length us, event | category | flops | bytes accessed | tf_op | source)
XLA Modules:
  0.0 37.6 jit_solution(17335674345900709387)
XLA Ops:
  0.0 35.6 %scores.1 = f32[512,384]{1,0:T(8,128)} custom-call(bf16[512,4096]{1,0:T(8,128)(2,1)} %train.1, bf16[24,4096]{1,0:T(8,128)(2,1)} %query.1, bf16[4,32,32]{2,1,0:T(8,128)(2,1)} %in_basis.1, bf16[4,32,32]{2,1,0:T(8,128)(2,1)} %out_basis.1, f32[2]{0:T(128)} %damping.1, s32[4]{0:T(128)} %layer_group.1), custom_call_target="tpu_custom_call" | custom-call | tf_op jit(solution)/shard_map/scores/pallas_call | solution.py:297
  35.6 2.1 %copy.8 = f32[512,384]{1,0:T(8,128)} copy(f32[512,384]{1,0:T(8,128)} %scores.1) | data formatting | bytes 1572864
